TPU v7x, 32 devices: a whole 2x2x4 slice. The times are simulated.
32 devices in a mesh: lang: 4 (over x, core), fsdp: 2 (over y), dp: 4 (over z).
Axes of the slice: x: 2, y: 2, z: 4, core: 2. Of those that a mesh axis runs over, the one named last changes fastest.
Arguments:
- tokens_in: bfloat16 [1024, 8192], P('dp'), may hold values from -6 to 6
- cotangent: bfloat16 [1024, 16384], P('dp', ('lang', 'fsdp')), may hold values from -6 to 6
- gate_base: bfloat16 [8192, 16384], P('dp', ('lang', 'fsdp')), may hold values from -0.0625 to 0.0625
- up_base: bfloat16 [8192, 16384], P('dp', ('lang', 'fsdp')), may hold values from -0.0625 to 0.0625
- lang_delta: bfloat16 [4, 2, 4, 4, 32768], P('lang', 'fsdp'), may hold values from -0.1796875 to 0.1796875
- lang_cell: int32 [4, 2, 4, 4], P('lang', 'fsdp'), may hold values from -1 to 1023, as said below
- group_lang: int32 [4], P('dp'), may hold values from 0 to 3
- task_delta: bfloat16 [128, 32768], P(('lang', 'fsdp')), may hold values from -0.1796875 to 0.1796875
- task_slab: int32 [128, 1], P(('lang', 'fsdp')), may hold values from 0 to 1; in each aligned block of 16 rows (0 to 15, 16 to 31, ...) at most 8 rows name the same one
- task_cell: int32 [128, 1], P(('lang', 'fsdp')), may hold values from 0 to 1023
Outputs:
- grad_input: bfloat16 [1024, 8192], P('dp', ('lang', 'fsdp'))
- task_grad: float32 [128, 32768], P(('lang', 'fsdp'))
Inputs may be any that keep to these rules, and one draw needn't show every extreme that they name: `lang_cell`: -1 marks an empty slot; every other entry is a cell of the slab. In every draw the list of slab 0 is full for every language. `task_slab`: among the 16 task blocks of one device, no slab is named more than 8 times; some slab is named exactly 8 times.
All inputs are finite; a program needn't handle non-finite values.
Results may differ from a plain program's by a relative error of at most 0.0063.
Values may be sent and summed in bfloat16 or wider, within the bound.
A program may use at most 448 MiB of HBM per device.

v0:
```python
import jax
import jax.numpy as jnp
from jax import lax
from jax.sharding import PartitionSpec as P

D = 8192
BLK = 128


def spread(value, axis, source):
    kept = jnp.where(lax.axis_index(axis) == source, value, 0).astype(value.dtype)
    return lax.psum(kept, axis)


def place_blocks(cell_ids, tile_vals, cell_total):
    one_hot = (cell_ids[:, None] == jnp.arange(cell_total, dtype=jnp.int32)[None, :]).astype(
        jnp.bfloat16
    )
    return lax.dot_general(
        one_hot, tile_vals, (((0,), (0,)), ((), ())), preferred_element_type=jnp.float32
    )


def on_device(
    tokens_in,
    cotangent,
    gate_base,
    up_base,
    lang_delta,
    lang_cell,
    group_lang,
    task_delta,
    task_slab,
    task_cell,
):
    tile_size = BLK * BLK
    slab_cols = gate_base.shape[1]
    slab_width = slab_cols // BLK
    row_blocks = D // BLK
    group_rows = tokens_in.shape[0]
    language = group_lang[0]
    range_index = lax.axis_index("lang")
    owner_vals, owner_cells = (
        spread(lang_delta, "lang", language),
        spread(lang_cell, "lang", language),
    )
    own_tiles = lax.dynamic_index_in_dim(owner_vals[0, 0], range_index, 0, keepdims=False)
    own_cells = lax.dynamic_index_in_dim(owner_cells[0, 0], range_index, 0, keepdims=False)
    fsdp_ways = lax.axis_size("fsdp")
    held = task_delta.shape[0]
    capacity = max(2, (held + fsdp_ways - 1) // fsdp_ways)
    target = task_slab[:, 0]
    matches = (target[:, None] == jnp.arange(fsdp_ways, dtype=jnp.int32)[None, :]).astype(jnp.int32)
    slot_of = jnp.sum(jnp.cumsum(matches, axis=0) * matches, axis=1) - 1
    send_vals = (
        jnp.zeros((fsdp_ways, capacity, 2 * tile_size), jnp.bfloat16)
        .at[target, slot_of]
        .set(task_delta)
    )
    send_cells = (
        jnp.full((fsdp_ways, capacity), -1, jnp.int32).at[target, slot_of].set(task_cell[:, 0])
    )
    got_vals, got_cells = (
        lax.all_to_all(send_vals, "fsdp", split_axis=0, concat_axis=0, tiled=True),
        lax.all_to_all(send_cells, "fsdp", split_axis=0, concat_axis=0, tiled=True),
    )
    base_gate, base_up = (
        lax.all_gather(gate_base, "dp", axis=0, tiled=True),
        lax.all_gather(up_base, "dp", axis=0, tiled=True),
    )
    slot_cells = got_cells.reshape(-1)
    all_cells = jnp.concatenate([own_cells, slot_cells])
    all_tiles = jnp.concatenate([own_tiles, got_vals.reshape(-1, 2 * tile_size)], axis=0)
    changes = place_blocks(all_cells, all_tiles, row_blocks * slab_width)
    changes = changes.reshape(row_blocks, slab_width, 2, BLK, BLK)

    def as_matrix(part_index):
        return changes[:, :, part_index].transpose(0, 2, 1, 3).reshape(D, slab_cols)

    gate_matrix = (base_gate.astype(jnp.float32) + as_matrix(0)).astype(jnp.bfloat16)
    up_matrix = (base_up.astype(jnp.float32) + as_matrix(1)).astype(jnp.bfloat16)
    gate_pre = jnp.dot(tokens_in, gate_matrix, preferred_element_type=jnp.float32)
    up_pre = jnp.dot(tokens_in, up_matrix, preferred_element_type=jnp.float32)
    sigmoid_g = jax.nn.sigmoid(gate_pre)
    upstream = cotangent.astype(jnp.float32)
    d_gate = (upstream * up_pre * sigmoid_g * (1.0 + gate_pre * (1.0 - sigmoid_g))).astype(
        jnp.bfloat16
    )
    d_up = (upstream * gate_pre * sigmoid_g).astype(jnp.bfloat16)
    contract = (((1,), (1,)), ((), ()))
    partial_g = lax.dot_general(gate_matrix, d_gate, contract, preferred_element_type=jnp.float32)
    summed = lax.psum_scatter(
        partial_g + lax.dot_general(up_matrix, d_up, contract, preferred_element_type=jnp.float32),
        ("lang", "fsdp"),
        scatter_dimension=0,
        tiled=True,
    )
    grad_input = summed.T.astype(jnp.bfloat16)
    filled = slot_cells >= 0
    clamped = jnp.where(filled, slot_cells, 0)
    x_tiles = tokens_in.reshape(group_rows, row_blocks, BLK)[:, clamped // slab_width, :]
    g_tiles = d_gate.reshape(group_rows, slab_width, BLK)[:, clamped % slab_width, :]
    u_tiles = d_up.reshape(group_rows, slab_width, BLK)[:, clamped % slab_width, :]
    gate_grad = jnp.einsum("tmi,tmj->mij", x_tiles, g_tiles, preferred_element_type=jnp.float32)
    up_grad = jnp.einsum("tmi,tmj->mij", x_tiles, u_tiles, preferred_element_type=jnp.float32)
    slot_grads = jnp.concatenate(
        [gate_grad.reshape(-1, tile_size), up_grad.reshape(-1, tile_size)], axis=1
    )
    slot_grads = jnp.where(filled[:, None], slot_grads, 0.0).reshape(
        fsdp_ways, capacity, 2 * tile_size
    )
    slot_grads = lax.psum(slot_grads, "dp")
    returned = lax.all_to_all(slot_grads, "fsdp", split_axis=0, concat_axis=0, tiled=True)
    task_grad = returned[target, slot_of]
    return (grad_input, task_grad)


def solution(mesh):
    return jax.shard_map(
        on_device,
        mesh=mesh,
        in_specs=(
            P("dp", None),
            P("dp", ("lang", "fsdp")),
            P("dp", ("lang", "fsdp")),
            P("dp", ("lang", "fsdp")),
            P("lang", "fsdp", None, None, None),
            P("lang", "fsdp", None, None),
            P("dp"),
            P(("lang", "fsdp"), None),
            P(("lang", "fsdp"), None),
            P(("lang", "fsdp"), None),
        ),
        out_specs=(P("dp", ("lang", "fsdp")), P(("lang", "fsdp"), None)),
        check_vma=False,
    )
```

profile of v0, /device:TPU:2, one launch (start us, length us, event | category | flops | bytes accessed | tf_op | source)
XLA Modules:
  0.0 1370.6 jit_solution(10713854699882259890)
XLA Ops:
  8.7 1.4 broadcast_select_fusion
  10.2 0.5 all-gather.3.cloned.1.call-update
  10.8 0.5 all-gather.5.cloned.1.call-update
  11.4 0.2 select_reduce_fusion
  11.6 0.6 fusion.22
  12.2 0.6 broadcast.200
  12.7 2.9 scatter_fusion
  15.7 3.2 all-to-all-start
  18.9 1.3 copy.47
  20.2 7.2 copy.49
  27.4 6.8 copy.50
  34.2 1.0 broadcast_in_dim.26
  35.2 23.0 %scatter_fusion.1 = bf16[2,8,32768]{2,1,0:T(8,128)(2,1)} fusion(bf16[2,8,32768]{2,1,0:T(8,128)(2,1)} %broadcast_in_dim.26, s32[16]{0:T(128)S(1)} %get-tuple-element.14, bf16[16,32768]{1,0:T(8,128)(2,1)S(1)} %copy-done.2), kind=kCustom, calls=%fused_computation.5 | custom fusion | bytes 3145856 | tf_op jit(solution)/shard_map/scatter | solution.py:58
  58.2 4.8 psum.21
  63.0 3.6 all-to-all-start.1
  66.7 0.5 broadcast.316
  67.2 0.7 reduce.5
  68.1 0.5 copy.71
  68.6 3.8 gather_fusion
  72.5 0.6 pad_clamp_fusion
  73.1 1.0 dynamic-slice_bitcast_fusion
  74.2 6.1 all-to-all-done.1
  80.3 45.3 %convolution_bitcast_fusion = f32[128,8,256,128]{3,1,2,0:T(8,128)} fusion(bf16[16,32768]{1,0:T(8,128)(2,1)S(1)} %bitcast.102, bf16[4,32768]{1,0:T(4,128)(2,1)S(1)} %dynamic-slice_bitcast_fusion, s32[20]{0:T(128)S(1)} %pad_add_fusion), kind=kOutput, calls=%fused_computation.12 | convolution fusion | flops 1344819200 | bytes 135528528 | tf_op jit(solution)/shard_map/dot_general | solution.py:19
  125.6 88.8 %copy.59 = f32[128,8,256,128]{3,2,1,0:T(8,128)} copy(f32[128,8,256,128]{3,1,2,0:T(8,128)} %convolution_bitcast_fusion) | data formatting | bytes 268435456
  214.4 84.8 %slice_bitcast_fusion = (f32[64,128,16,128]{3,1,2,0:T(8,128)}, f32[64,128,16,128]{3,1,2,0:T(8,128)}) fusion(f32[64,16,2,128,128]{4,3,2,1,0:T(8,128)} %bitcast.34), kind=kLoop, calls=%fused_computation.10 | loop fusion | bytes 268435456 | tf_op jit(solution)/shard_map/transpose | solution.py:78
  299.2 56.3 %copy.46 = f32[64,128,16,128]{3,2,1,0:T(8,128)} copy(f32[64,128,16,128]{3,1,2,0:T(8,128)} %get-tuple-element.17) | data formatting | bytes 134217728 | tf_op jit(solution)/shard_map/transpose | solution.py:78
  355.5 56.5 %copy.48 = f32[64,128,16,128]{3,2,1,0:T(8,128)} copy(f32[64,128,16,128]{3,1,2,0:T(8,128)} %get-tuple-element.16) | data formatting | bytes 134217728 | tf_op jit(solution)/shard_map/transpose | solution.py:78
  412.0 162.8 %all-gather.3.cloned.1.call-done = bf16[8192,2048]{1,0:T(8,128)(2,1)} async-done(((bf16[2048,2048]{1,0:T(8,128)(2,1)}), bf16[8192,2048]{1,0:T(8,128)(2,1)}) %all-gather.3.cloned.1.call-update) | async-done | bytes 33554448 | tf_op jit(solution)/shard_map/all_gather | solution.py:68
  574.8 52.4 %fusion.7 = (bf16[256,2048]{0,1:T(8,128)(2,1)S(1)}, f32[256,2048]{0,1:T(8,128)}) fusion(bf16[256,2048]{0,1:T(8,128)(2,1)S(1)} %copy-done, bf16[256,8192]{1,0:T(8,128)(2,1)} %param.10, f32[1024,8,16,128]{3,2,1,0:T(8,128)} %bitcast.36, bf16[8192,2048]{1,0:T(8,128)(2,1)} %all-gather.3.cloned.1.call-done), kind=kOutput, calls=%fused_computation.22 | convolution fusion | flops 8643936256 | bytes 109051904 | tf_op jit(solution)/shard_map/dot_general | solution.py:82
  627.2 508.6 %all-gather.5.cloned.1.call-done = bf16[8192,2048]{1,0:T(8,128)(2,1)} async-done(((bf16[2048,2048]{1,0:T(8,128)(2,1)}), bf16[8192,2048]{1,0:T(8,128)(2,1)}) %all-gather.5.cloned.1.call-update) | async-done | bytes 33554448 | tf_op jit(solution)/shard_map/all_gather | solution.py:69
  1135.7 48.3 %fusion.5 = bf16[256,2048]{0,1:T(8,128)(2,1)S(1)} fusion(bf16[256,8192]{1,0:T(8,128)(2,1)} %param.10, bf16[256,2048]{0,1:T(8,128)(2,1)S(1)} %copy-done, f32[256,2048]{0,1:T(8,128)} %get-tuple-element.19, f32[1024,8,16,128]{3,2,1,0:T(8,128)} %bitcast.39, bf16[8192,2048]{1,0:T(8,128)(2,1)} %all-gather.5.cloned.1.call-done), kind=kOutput, calls=%fused_computation.20 | convolution fusion | flops 8646033408 | bytes 109051904 | tf_op jit(solution)/shard_map/dot_general | solution.py:83
  1184.1 1.3 copy.51
  1185.4 3.0 gather_fusion.1
  1188.4 3.0 fusion.13
  1191.4 2.4 concatenate.22
  1193.8 1.3 copy.53
  1195.1 3.1 gather_fusion.2
  1198.1 2.7 fusion.11
  1200.8 1.4 concatenate.23
  1202.2 2.7 maximum_select_fusion
  1205.1 40.3 %fusion.24 = f32[8192,256]{1,0:T(8,128)} fusion(bf16[256,2048]{0,1:T(8,128)(2,1)S(1)} %fusion.5, f32[1024,8,16,128]{3,2,1,0:T(8,128)} %bitcast.36, bf16[8192,2048]{1,0:T(8,128)(2,1)} %all-gather.3.cloned.1.call-done), kind=kOutput, calls=%fused_computation.67 | convolution fusion | flops 8640266240 | bytes 110100480 | tf_op jit(solution)/shard_map/dot_general | solution.py:91
  1245.4 42.0 %convolution_add_fusion = f32[8192,256]{1,0:T(8,128)} fusion(f32[8192,256]{1,0:T(8,128)} %fusion.24, bf16[256,2048]{0,1:T(8,128)(2,1)S(1)} %get-tuple-element.18, f32[1024,8,16,128]{3,2,1,0:T(8,128)} %bitcast.39, bf16[8192,2048]{1,0:T(8,128)(2,1)} %all-gather.5.cloned.1.call-done), kind=kOutput, calls=%fused_computation.13 | convolution fusion | flops 8642363392 | bytes 118489088 | tf_op jit(solution)/shard_map/dot_general | solution.py:93
  1287.4 1.9 all-reduce.5.cloned.1.call-done
  1289.3 35.3 %all_to_all.19 = f32[2,8,32768]{2,1,0:T(8,128)S(1)} all-to-all(f32[2,8,32768]{2,1,0:T(8,128)} %all-reduce.5.cloned.1.call-done), channel_id=1, replica_groups=mesh['lang'=4,'fsdp'=2,'dp'=4] {'fsdp'}, dimensions={0} | all-to-all | bytes 4194304 | tf_op jit(solution)/shard_map/all_to_all | solution.py:113
  1324.6 3.3 gather_fusion.3
  1327.9 32.4 %reduce-scatter.2.cloned.1.call-done = f32[1024,256]{1,0:T(8,128)} async-done(((f32[8192,256]{1,0:T(8,128)}), f32[1024,256]{1,0:T(8,128)}) %reduce-scatter.2.cloned.1.call-update) | async-done | bytes 1048592 | tf_op jit(solution)/shard_map/reduce_scatter | solution.py:92
  1360.3 1.3 convert_bitcast_fusion
  1361.6 1.0 copy.55
  (39 shorter events, 0.7 us)
Async XLA Ops:
  8.0 65.1 %all-reduce.3.cloned.1.call-start = ((), (), s32[]{:S(2)}) async-start(), calls=%async_computation.5 | async-start | bytes 2097152 | tf_op jit(solution)/shard_map/psum | solution.py:12
  10.1 1.2 copy-start.5
  10.1 2.6 copy-start.7
  10.1 8.7 copy-start.3
  10.1 564.6 %all-gather.3.cloned.1.call-start = ((), (), s32[]{:S(2)}) async-start(), calls=%async_computation.4 | async-start | bytes 41943040 | tf_op jit(solution)/shard_map/all_gather | solution.py:68
  10.7 1125.0 %all-gather.5.cloned.1.call-start = ((), (), s32[]{:S(2)}) async-start(), calls=%async_computation.6 | async-start | bytes 41943040 | tf_op jit(solution)/shard_map/all_gather | solution.py:69
  15.7 47.4 %all-to-all-start = ((s32[2,1,8]{2,1,0:T(1,128)}), s32[2,1,8]{2,1,0:T(1,128)S(1)}, u32[]{:S(2)}, u32[]{:S(2)}) async-start(s32[2,1,8]{2,1,0:T(1,128)} %bitcast.8), calls=%async_computation | async-start | bytes 2048 | tf_op jit(solution)/shard_map/all_to_all | solution.py:65
  20.2 15.0 %copy-start.2 = (bf16[16,32768]{1,0:T(8,128)(2,1)S(1)}, bf16[16,32768]{1,0:T(8,128)(2,1)}, u32[]{:S(2)}) copy-start(bf16[16,32768]{1,0:T(8,128)(2,1)} %param.17) | copy-start | bytes 3145732
  35.2 23.0 %copy-start.6 = (s32[1,1,4,4]{3,2,1,0:T(4,128)S(1)}, s32[1,1,4,4]{3,2,1,0:T(4,128)}, u32[]{:S(2)}) copy-start(s32[1,1,4,4]{3,2,1,0:T(4,128)} %param.15) | copy-start | bytes 196
  63.0 17.3 %all-to-all-start.1 = ((bf16[2,8,32768]{2,1,0:T(8,128)(2,1)}), bf16[2,8,32768]{2,1,0:T(8,128)(2,1)S(1)}, u32[]{:S(2)}, u32[]{:S(2)}) async-start(bf16[2,8,32768]{2,1,0:T(8,128)(2,1)} %scatter_fusion.1), calls=%async_computation.1 | async-start | bytes 2097152 | tf_op jit(solution)/shard_map/all_to_all | solution.py:64
  66.6 1222.6 %all-reduce.5.cloned.1.call-start = ((), (), s32[]{:S(2)}) async-start(), calls=%async_computation.8 | async-start | bytes 4194304 | tf_op jit(solution)/shard_map/psum | solution.py:112
  355.5 219.2 %copy-start = (bf16[256,2048]{0,1:T(8,128)(2,1)S(1)}, bf16[256,2048]{0,1:T(8,128)(2,1)}, u32[]{:S(2)}) copy-start(bf16[256,2048]{0,1:T(8,128)(2,1)} %copy.47) | copy-start | bytes 3145732
  1184.1 14.1 %copy-start.1 = (bf16[16,256,128]{2,1,0:T(8,128)(2,1)S(1)}, bf16[16,256,128]{2,1,0:T(8,128)(2,1)}, u32[]{:S(2)}) copy-start(bf16[16,256,128]{2,1,0:T(8,128)(2,1)} %gather_fusion) | copy-start | bytes 3145732
  1185.4 16.8 %copy-start.8 = (pred[2,1,8]{2,0,1:T(4,128)(4,1)S(1)}, pred[2,1,8]{2,0,1:T(4,128)(4,1)}, u32[]{:S(2)}) copy-start(pred[2,1,8]{2,0,1:T(4,128)(4,1)} %copy.71) | copy-start | bytes 52
  1205.0 155.3 %reduce-scatter.2.cloned.1.call-start = ((), (), s32[]{:S(2)}) async-start(), calls=%async_computation.7 | async-start | bytes 9437184 | tf_op jit(solution)/shard_map/reduce_scatter | solution.py:92
  1287.4 37.2 %copy-start.4 = (s32[16,1]{0,1:T(1,128)S(1)}, s32[16,1]{0,1:T(1,128)}, u32[]{:S(2)}) copy-start(s32[16,1]{0,1:T(1,128)} %get-tuple-element.15) | copy-start | bytes 196
Sparse Core Ops, SparseCore 0:
  11.2 36.8 all-reduce.2
  1287.5 72.7 reduce-scatter.1
Sparse Core Ops, SparseCore 1:
  12.3 562.4 all-gather.2
  576.3 559.4 all-gather.4
  1205.1 84.1 all-reduce.4
where the time goes:
time: 1380 us; the launch traced here: 1370 us
  waiting for transfers between devices  713 us (52%)
  local copies, waits for them, and re-layouts  352 us (26%)
  matrix products  234 us (17%)
  blocking collectives  40.1 us (3%)
  between operations  16.9 us (1%)
    all_gather x1, waiting for transfers between devices, on_device(): lax.all_gather(up_base, 'dp', axis=0, tiled=True)  509 us
    transpose x3, local copies, waits for them, and re-layouts, as_matrix(): return changes[:, :, part_index].transpose(0, 2, 1, 3).reshape(D, slab_cols)  198 us
    all_gather x1, waiting for transfers between devices, on_device(): lax.all_gather(gate_base, 'dp', axis=0, tiled=True)  163 us
    unnamed x23, local copies, waits for them, and re-layouts  98.8 us
    dot_general x1, matrix products, on_device(): jnp.dot(tokens_in, gate_matrix, preferred_element_type=jnp.float32)  52.4 us
    dot_general x1, matrix products, on_device(): up_pre = jnp.dot(tokens_in, up_matrix, preferred_element_type=jnp.float32)  48.3 us
    dot_general x1, matrix products, place_blocks(): lax.dot_general(one_hot, tile_vals, (((0,), (0,)), ((), ())), preferred_e...  45.3 us
    dot_general x1, matrix products, on_device(): lax.dot_general(up_matrix, d_up, contract, preferred_element_type=jnp.flo...  42 us
  transfers between devices with their start and end apart: 7, of which 5 were waited for; matrix products, arithmetic and copies ran while one was open for 38% of the time, Pallas kernels for 0%

commit v1 on v0

v1 whole, which is shorter than its diff:
```python
import jax
import jax.numpy as jnp
from jax import lax
from jax.sharding import PartitionSpec as P

D = 8192
BLK = 128
F32 = jnp.float32
BF16 = jnp.bfloat16


def on_device(
    tokens_in,
    cotangent,
    gate_base,
    up_base,
    lang_delta,
    lang_cell,
    group_lang,
    task_delta,
    task_slab,
    task_cell,
):
    tile_size = BLK * BLK
    own_rows, slab_cols = gate_base.shape
    slab_width = slab_cols // BLK
    row_blocks = D // BLK
    own_blocks = own_rows // BLK
    group_rows = tokens_in.shape[0]
    lang_ways, fsdp_ways = lax.axis_size("lang"), lax.axis_size("fsdp")
    groups = lax.axis_size("dp")
    plane = lang_ways * fsdp_ways
    part = lax.axis_index("dp")
    place = lax.axis_index("lang") * fsdp_ways + lax.axis_index("fsdp")

    piece = own_rows // plane
    mine = lax.dynamic_index_in_dim(
        tokens_in.reshape(group_rows, groups, plane, piece), place, 2, keepdims=False
    )
    mine = lax.all_to_all(mine, "dp", split_axis=1, concat_axis=0, tiled=True)
    x_all = lax.all_gather(
        mine.reshape(groups * group_rows, piece), ("lang", "fsdp"), axis=1, tiled=True
    )

    held = task_delta.shape[0]
    capacity = max(2, (held + fsdp_ways - 1) // fsdp_ways)
    target = task_slab[:, 0]
    matches = (target[:, None] == jnp.arange(fsdp_ways, dtype=jnp.int32)[None, :]).astype(jnp.int32)
    slot_of = jnp.sum(jnp.cumsum(matches, axis=0) * matches, axis=1) - 1
    taken = (matches.T[:, None, :] == 1) & (
        slot_of[None, None, :] == jnp.arange(capacity, dtype=jnp.int32)[None, :, None]
    )
    source = jnp.argmax(taken, axis=2)
    send_vals = task_delta[source.reshape(-1)].reshape(fsdp_ways, capacity, 2 * tile_size)
    send_cells = jnp.where(jnp.any(taken, axis=2), task_cell[:, 0][source], -1)
    got_vals = lax.all_to_all(send_vals, "fsdp", split_axis=0, concat_axis=0, tiled=True)
    got_cells = lax.all_to_all(send_cells, "fsdp", split_axis=0, concat_axis=0, tiled=True)

    lang_vals = lax.all_to_all(lang_delta[0, 0], "lang", split_axis=0, concat_axis=0, tiled=True)
    lang_cells = lax.all_to_all(lang_cell[0, 0], "lang", split_axis=0, concat_axis=0, tiled=True)
    languages = lax.all_gather(group_lang, "dp", axis=0, tiled=True)
    per_lang = lang_cells.shape[1]

    task_cells = got_cells.reshape(-1)
    tiles = jnp.concatenate(
        [got_vals.reshape(-1, 2 * tile_size), lang_vals.reshape(-1, 2 * tile_size)], axis=0
    )
    gate_tiles = tiles[:, :tile_size].reshape(-1, BLK, BLK)
    up_tiles = tiles[:, tile_size:].reshape(-1, BLK, BLK)
    cells = jnp.concatenate([task_cells, lang_cells.reshape(-1)])
    task_slots = task_cells.shape[0]
    lang_of = jnp.concatenate(
        [
            jnp.full((task_slots,), -1, jnp.int32),
            jnp.repeat(jnp.arange(lang_ways, dtype=jnp.int32), per_lang),
        ]
    )
    counted = (cells >= 0)[:, None] & (
        (lang_of < 0)[:, None] | (lang_of[:, None] == languages[None, :])
    )
    safe = jnp.where(cells >= 0, cells, 0)
    row_of, col_of = safe // slab_width, safe % slab_width

    def frozen(weights):
        partial = jnp.dot(x_all, weights, preferred_element_type=F32).astype(BF16)
        return lax.psum_scatter(partial, "dp", scatter_dimension=0, tiled=True).astype(F32)

    gate_frozen, up_frozen = frozen(gate_base), frozen(up_base)

    x_slots = tokens_in.reshape(group_rows, row_blocks, BLK).transpose(1, 0, 2)[row_of]
    counted_here = lax.dynamic_index_in_dim(counted, part, 1, keepdims=False)
    to_cols = (
        counted_here[:, None]
        & (col_of[:, None] == jnp.arange(slab_width, dtype=jnp.int32)[None, :])
    ).astype(BF16)

    def blocks_part(block_tiles):
        products = jnp.einsum(
            "kti,kij->ktj", x_slots, block_tiles, preferred_element_type=F32
        ).astype(BF16)
        placed = jnp.einsum("kc,ktj->ctj", to_cols, products, preferred_element_type=F32)
        return placed.transpose(1, 0, 2).reshape(group_rows, slab_cols)

    gate_pre = gate_frozen + blocks_part(gate_tiles)
    up_pre = up_frozen + blocks_part(up_tiles)
    sigmoid_g = jax.nn.sigmoid(gate_pre)
    upstream = cotangent.astype(F32)
    d_gate = (upstream * up_pre * sigmoid_g * (1.0 + gate_pre * (1.0 - sigmoid_g))).astype(BF16)
    d_up = (upstream * gate_pre * sigmoid_g).astype(BF16)
    g_all = lax.all_gather(d_gate, "dp", axis=0, tiled=True)
    u_all = lax.all_gather(d_up, "dp", axis=0, tiled=True)

    tokens = groups * group_rows
    g_slots = g_all.reshape(tokens, slab_width, BLK).transpose(1, 0, 2)[col_of]
    u_slots = u_all.reshape(tokens, slab_width, BLK).transpose(1, 0, 2)[col_of]
    own_row = row_of - part * own_blocks
    at_row = own_row[:, None] == jnp.arange(own_blocks, dtype=jnp.int32)[None, :]
    to_rows = (counted[:, :, None] & at_row[:, None, :]).astype(BF16)
    products = jnp.einsum("ktj,kij->kti", g_slots, gate_tiles, preferred_element_type=F32)
    products = products + jnp.einsum("ktj,kij->kti", u_slots, up_tiles, preferred_element_type=F32)
    products = products.astype(BF16).reshape(-1, groups, group_rows, BLK)
    placed = jnp.einsum("kgr,kgti->grti", to_rows, products, preferred_element_type=F32)
    contract = (((1,), (1,)), ((), ()))
    total = lax.dot_general(g_all, gate_base, contract, preferred_element_type=F32)
    total = total + lax.dot_general(u_all, up_base, contract, preferred_element_type=F32)
    total = total + placed.transpose(0, 2, 1, 3).reshape(tokens, own_rows)

    out_cols = own_rows // fsdp_ways
    total = total.reshape(groups, group_rows, fsdp_ways, out_cols).transpose(0, 2, 1, 3)
    summed = lax.psum_scatter(
        total.reshape(plane, group_rows, out_cols),
        ("lang", "fsdp"),
        scatter_dimension=0,
        tiled=True,
    )[0].astype(BF16)
    swap = [(l * groups + p, p * groups + l) for l in range(lang_ways) for p in range(groups)]
    grad_input = lax.ppermute(summed, ("lang", "dp"), swap)

    here = (task_cells >= 0) & jnp.any(at_row[:task_slots], axis=1)
    local_row = jnp.clip(own_row[:task_slots], 0, own_blocks - 1)
    x_tiles = x_all.reshape(tokens, own_blocks, BLK).transpose(1, 0, 2)[local_row]
    gate_grad = jnp.einsum("kti,ktj->kij", x_tiles, g_slots[:task_slots], preferred_element_type=F32)
    up_grad = jnp.einsum("kti,ktj->kij", x_tiles, u_slots[:task_slots], preferred_element_type=F32)
    slot_grads = jnp.stack([gate_grad, up_grad], axis=1)
    slot_grads = jnp.where(here[:, None, None, None], slot_grads, 0.0).astype(BF16)
    slot_grads = slot_grads.reshape(fsdp_ways, capacity, 2 * tile_size)
    slot_grads = lax.psum(slot_grads, "dp")
    returned = lax.all_to_all(slot_grads, "fsdp", split_axis=0, concat_axis=0, tiled=True)
    task_grad = returned[target, slot_of].astype(F32)
    return (grad_input, task_grad)


def solution(mesh):
    return jax.shard_map(
        on_device,
        mesh=mesh,
        in_specs=(
            P("dp", None),
            P("dp", ("lang", "fsdp")),
            P("dp", ("lang", "fsdp")),
            P("dp", ("lang", "fsdp")),
            P("lang", "fsdp", None, None, None),
            P("lang", "fsdp", None, None),
            P("dp"),
            P(("lang", "fsdp"), None),
            P(("lang", "fsdp"), None),
            P(("lang", "fsdp"), None),
        ),
        out_specs=(P("dp", ("lang", "fsdp")), P(("lang", "fsdp"), None)),
        check_vma=False,
    )
```

time: 1380 us -> 633 us (0.46)
  waiting for transfers between devices: 713 us -> 339 us
  local copies, waits for them, and re-layouts: 352 us -> 96.4 us
  matrix products: 234 us -> 102 us
  starting transfers between devices: 7 us -> 22.5 us
    all_gather x2 -> x3, waiting for transfers between devices: 671 us -> 167 us  [the longest x1 68 us: on_device(): g_all = lax.all_gather(d_gate, 'dp', axis=0, tiled=True)]
    transpose x3, local copies, waits for them, and re-layouts: 198 us -> 19.6 us  [the longest x1 9.16 us: on_device(): total.reshape(groups, group_rows, fsdp_ways, out_cols).transpose(0, 2, 1, 3)]
    dot_general x7 -> x13, matrix products: 234 us -> 102 us  [the longest x2 27.7 us: frozen(): partial = jnp.dot(x_all, weights, preferred_element_type=F32).astype(BF16)]
    reduce_scatter x1 -> x3, waiting for transfers between devices: 32.4 us -> 140 us  [the longest x2 73.9 us: frozen(): lax.psum_scatter(partial, 'dp', scatter_dimension=0, tiled=True).astype(F32)]
    unnamed x23 -> x33, local copies, waits for them, and re-layouts: 98.8 us -> 10.8 us
    scatter x2 -> x0, local copies, waits for them, and re-layouts: 25.9 us -> none  [the longest x1 23 us: on_device(): send_vals = jnp.zeros((fsdp_ways, capacity, 2 * tile_size), jnp.bfloat16)...]
    ppermute x0 -> x1, waiting for transfers between devices: none -> 19.7 us  [on_device(): grad_input = lax.ppermute(summed, ('lang', 'dp'), swap)]
    reshape x5 -> x6, local copies, waits for them, and re-layouts: 9.55 us -> 26.9 us  [the longest x1 11.7 us: on_device(): total.reshape(groups, group_rows, fsdp_ways, out_cols).transpose(0, 2, 1, 3)]
  transfers between devices with their start and end apart: 7 -> 12, of which waited for: 5 -> 8; matrix products, arithmetic and copies ran while one was open for 38% -> 25% of each run, Pallas kernels for 0% -> 0%
where the time goes in v1:
time: 633 us; the launch traced here: 624 us
  waiting for transfers between devices  339 us (54%)
  matrix products  102 us (16%)
  local copies, waits for them, and re-layouts  96.4 us (15%)
  blocking collectives  32.9 us (5%)
  starting transfers between devices  22.5 us (4%)
  other arithmetic  15.8 us (2%)
  between operations  15.6 us (2%)
    reduce_scatter x2, waiting for transfers between devices, frozen(): lax.psum_scatter(partial, 'dp', scatter_dimension=0, tiled=True).astype(F32)  73.9 us
    all_gather x1, waiting for transfers between devices, on_device(): g_all = lax.all_gather(d_gate, 'dp', axis=0, tiled=True)  68 us
    reduce_scatter x1, waiting for transfers between devices, on_device(): lax.psum_scatter(total.reshape(plane, group_rows, out_cols), ('lang', 'fs...  66.3 us
    all_gather x1, waiting for transfers between devices, on_device(): u_all = lax.all_gather(d_up, 'dp', axis=0, tiled=True)  62.4 us
    all_gather x1, waiting for transfers between devices, on_device(): lax.all_gather(mine.reshape(groups * group_rows, piece), ('lang', 'fsdp')...  36.6 us
    dot_general x2, matrix products, frozen(): partial = jnp.dot(x_all, weights, preferred_element_type=F32).astype(BF16)  27.7 us
    dot_general x1, matrix products, on_device(): lax.dot_general(u_all, up_base, contract, preferred_element_type=F32)  20 us
    ppermute x1, waiting for transfers between devices, on_device(): grad_input = lax.ppermute(summed, ('lang', 'dp'), swap)  19.7 us
  transfers between devices with their start and end apart: 12, of which 8 were waited for; matrix products, arithmetic and copies ran while one was open for 25% of the time, Pallas kernels for 0%

profile of v1, /device:TPU:2, one launch (start us, length us, event | category | flops | bytes accessed | tf_op | source)
XLA Modules:
  0.0 624.1 jit_solution(8334640889883339514)
XLA Ops:
  7.2 6.5 %copy.70 = bf16[256,8192]{0,1:T(8,128)(2,1)} copy(bf16[256,8192]{1,0:T(8,128)(2,1)} %param.10) | data formatting | bytes 8388608 | tf_op args[0]
  15.0 19.3 %all_to_all.45 = bf16[256,4,256]{2,0,1:T(8,128)(2,1)} all-to-all(bf16[256,4,256]{2,0,1:T(8,128)(2,1)S(1)} %bitcast.144), channel_id=1, replica_groups=mesh['lang'=4,'fsdp'=2,'dp'=4] {'dp'}, dimensions={1} | all-to-all | bytes 1048576 | tf_op jit(solution)/shard_map/all_to_all | solution.py:40
  34.3 36.6 %all-gather.4.cloned.1.call-done = bf16[1024,2048]{1,0:T(8,128)(2,1)} async-done(((bf16[1024,256]{1,0:T(8,128)(2,1)}), bf16[1024,2048]{1,0:T(8,128)(2,1)}) %all-gather.4.cloned.1.call-update) | async-done | bytes 4194320 | tf_op jit(solution)/shard_map/all_gather | solution.py:41
  70.9 13.8 %convolution_convert_fusion.1 = bf16[1024,2048]{1,0:T(8,128)(2,1)} fusion(bf16[1024,2048]{1,0:T(8,128)(2,1)} %all-gather.4.cloned.1.call-done, bf16[2048,2048]{1,0:T(8,128)(2,1)} %param.13), kind=kOutput, calls=%fused_computation.18 | convolution fusion | flops 8592031744 | bytes 16777216 | tf_op jit(solution)/shard_map/dot_general | solution.py:85
  84.8 13.9 %convolution_convert_fusion = bf16[1024,2048]{1,0:T(8,128)(2,1)} fusion(bf16[1024,2048]{1,0:T(8,128)(2,1)} %all-gather.4.cloned.1.call-done, bf16[2048,2048]{1,0:T(8,128)(2,1)} %param.12), kind=kOutput, calls=%fused_computation.17 | convolution fusion | flops 8592031744 | bytes 16777216 | tf_op jit(solution)/shard_map/dot_general | solution.py:85
  101.9 3.2 all-to-all-start.1
  107.2 1.6 all-to-all-done.1
  108.8 4.8 all_to_all.46
  113.6 6.2 all-to-all-start.4
  119.8 8.8 %all-reduce.1 = s32[4]{0:T(128)S(1)} all-reduce(s32[4]{0:T(128)S(1)} %dynamic-update-slice), channel_id=1, replica_groups=mesh['lang'=4,'fsdp'=2,'dp'=4] {'dp'}, use_global_device_ids=true, to_apply=%add.1 | all-reduce | flops 4 | bytes 32
  128.7 6.4 %copy.75 = bf16[256,64,128]{2,0,1:T(8,128)(2,1)} copy(bf16[256,64,128]{0,2,1:T(8,128)(2,1)} %bitcast.131) | data formatting | bytes 8388608 | tf_op jit(solution)/shard_map/reshape | solution.py:90
  135.1 2.3 gather_fusion.2
  139.7 3.1 gather_fusion.1
  143.0 3.6 all-to-all-start.3
  147.3 2.2 reshape.498
  149.4 9.8 %all-to-all-done.3 = bf16[2,8,32768]{2,1,0:T(8,128)(2,1)S(1)} async-done(((bf16[2,8,32768]{2,1,0:T(8,128)(2,1)}), bf16[2,8,32768]{2,1,0:T(8,128)(2,1)S(1)}, u32[]{:S(2)}, u32[]{:S(2)}) %all-to-all-start.3) | async-done | bytes 1048608 | tf_op jit(solution)/shard_map/all_to_all | solution.py:56
  159.2 1.4 fusion.23
  161.8 2.6 fusion.13
  165.1 2.6 fusion.11
  167.7 73.9 %reduce-scatter.6.cloned.1.call-done = bf16[256,2048]{1,0:T(8,128)(2,1)} async-done(((bf16[1024,2048]{1,0:T(8,128)(2,1)}), bf16[256,2048]{1,0:T(8,128)(2,1)}) %reduce-scatter.6.cloned.1.call-update) | async-done | bytes 1048592 | tf_op jit(solution)/shard_map/reduce_scatter | solution.py:86
  241.5 6.2 fusion.10
  248.7 6.4 %copy.82 = bf16[1024,2048]{0,1:T(8,128)(2,1)} copy(bf16[1024,2048]{1,0:T(8,128)(2,1)} %all-gather.4.cloned.1.call-done) | data formatting | bytes 8388608 | tf_op jit(solution)/shard_map/all_gather | solution.py:41
  255.2 6.5 %copy.83 = bf16[1024,16,128]{2,0,1:T(8,128)(2,1)} copy(bf16[1024,16,128]{0,2,1:T(8,128)(2,1)} %bitcast.134) | data formatting | bytes 8388608 | tf_op jit(solution)/shard_map/reshape | solution.py:141
  261.6 5.2 gather_fusion.5
  266.8 62.4 %all-gather.8.cloned.1.call-done = bf16[1024,2048]{1,0:T(8,128)(2,1)} async-done(((bf16[256,2048]{1,0:T(8,128)(2,1)}), bf16[1024,2048]{1,0:T(8,128)(2,1)}) %all-gather.8.cloned.1.call-update) | async-done | bytes 4194320 | tf_op jit(solution)/shard_map/all_gather | solution.py:111
  329.2 5.2 bitcast_bitcast_fusion
  334.4 7.5 %gather_fusion.4 = bf16[32,1024,128]{2,1,0:T(8,128)(2,1)} fusion(bf16[16,1024,128]{2,1,0:T(8,128)(2,1)} %bitcast_bitcast_fusion, s32[1024]{0:T(1024)S(1)} %pad_clamp_fusion.1), kind=kCustom, calls=%fused_computation.4 | custom fusion | bytes 16777344 | tf_op jit(solution)/shard_map/gather | solution.py:115
  342.0 68.0 %all-gather.6.cloned.1.call-done = bf16[1024,2048]{1,0:T(8,128)(2,1)} async-done(((bf16[256,2048]{1,0:T(8,128)(2,1)}), bf16[1024,2048]{1,0:T(8,128)(2,1)}) %all-gather.6.cloned.1.call-update) | async-done | bytes 4194320 | tf_op jit(solution)/shard_map/all_gather | solution.py:110
  409.9 5.2 bitcast_bitcast_fusion.1
  415.1 7.3 %gather_fusion.3 = bf16[32,1024,128]{2,1,0:T(8,128)(2,1)} fusion(bf16[16,1024,128]{2,1,0:T(8,128)(2,1)} %bitcast_bitcast_fusion.1, s32[1024]{0:T(1024)S(1)} %pad_clamp_fusion.1), kind=kCustom, calls=%fused_computation.3 | custom fusion | bytes 16777344 | tf_op jit(solution)/shard_map/gather | solution.py:114
  422.4 11.6 %fusion.48 = f32[32,1024,128]{2,1,0:T(8,128)} fusion(bf16[32,1024,128]{2,1,0:T(8,128)(2,1)} %gather_fusion.3, bf16[32,128,128]{2,1,0:T(8,128)(2,1)S(1)} %bitcast.138), kind=kOutput, calls=%fused_computation.111 | convolution fusion | flops 1073741824 | bytes 26214400 | tf_op jit(solution)/shard_map/ktj,kij->kti/dot_general | solution.py:119
  434.0 1.4 fusion.15
  435.4 3.6 fusion.18
  439.7 1.2 select_convert_fusion
  441.2 9.7 %add_convert_fusion = bf16[32,1024,128]{2,1,0:T(8,128)(2,1)S(1)} fusion(f32[32,1024,128]{2,1,0:T(8,128)} %fusion.48, bf16[32,1024,128]{2,1,0:T(8,128)(2,1)} %gather_fusion.4, bf16[32,128,128]{2,1,0:T(8,128)(2,1)S(1)} %bitcast.136), kind=kOutput, calls=%fused_computation.7 | convolution fusion | flops 1082130432 | bytes 34603008 | tf_op jit(solution)/shard_map/ktj,kij->kti/dot_general | solution.py:120
  451.0 8.0 %fusion = f32[4,16,256,128]{3,1,2,0:T(8,128)} fusion(bf16[32,4,256,128]{3,2,1,0:T(8,128)(2,1)S(1)} %bitcast.127, pred[32,16]{0,1:T(8,128)(4,1)S(1)} %iota_compare_fusion, pred[32,4]{0,1:T(4,128)(4,1)S(1)} %or_and_fusion), kind=kOutput, calls=%fused_computation.9 | convolution fusion | flops 134219776 | bytes 16777856 | tf_op jit(solution)/shard_map/kgr,kgti->grti/dot_general | solution.py:122
  459.0 13.4 %fusion.47 = f32[1024,2048]{1,0:T(8,128)} fusion(bf16[1024,2048]{1,0:T(8,128)(2,1)S(1)} %copy-done.8, bf16[2048,2048]{1,0:T(8,128)(2,1)} %param.12), kind=kOutput, calls=%fused_computation.110 | convolution fusion | flops 8589934592 | bytes 20971520 | tf_op jit(solution)/shard_map/dot_general | solution.py:124
  472.5 20.0 %bitcast_add_fusion = f32[1024,2048]{1,0:T(8,128)} fusion(f32[128,8,16,128]{3,2,1,0:T(8,128)S(1)} %bitcast.132, f32[1024,2048]{1,0:T(8,128)} %fusion.47, bf16[1024,2048]{1,0:T(8,128)(2,1)} %all-gather.8.cloned.1.call-done, bf16[2048,2048]{1,0:T(8,128)(2,1)} %param.13), kind=kOutput, calls=%fused_computation.8 | convolution fusion | flops 8594128896 | bytes 37748736 | tf_op jit(solution)/shard_map/dot_general | solution.py:125
  492.4 11.7 %reshape.507 = f32[4,256,2,1024]{3,2,1,0:T(2,128)} reshape(f32[1024,2048]{1,0:T(8,128)} %bitcast_add_fusion) | data formatting | bytes 16777216 | tf_op jit(solution)/shard_map/reshape | solution.py:129
  504.2 9.2 %copy.81 = f32[4,2,256,1024]{3,2,1,0:T(8,128)} copy(f32[4,2,256,1024]{3,1,2,0:T(2,128)} %bitcast.129) | data formatting | bytes 16777216 | tf_op jit(solution)/shard_map/transpose | solution.py:129
  513.4 3.6 all-to-all-start.5
  517.0 66.3 %reduce-scatter.8.cloned.1.call-done = f32[1,256,1024]{2,1,0:T(8,128)} async-done(((f32[8,256,1024]{2,1,0:T(8,128)}), f32[1,256,1024]{2,1,0:T(8,128)}) %reduce-scatter.8.cloned.1.call-update) | async-done | bytes 1048592 | tf_op jit(solution)/shard_map/reduce_scatter | solution.py:130
  583.3 2.1 convert_bitcast_fusion
  585.4 4.7 collective-permute-start
  590.1 3.6 gather_fusion.6
  593.7 1.5 convert_element_type.70
  595.1 19.7 %collective-permute-done = bf16[256,1024]{1,0:T(8,128)(2,1)} collective-permute-done((bf16[256,1024]{1,0:T(8,128)(2,1)}, bf16[256,1024]{1,0:T(8,128)(2,1)}, u32[]{:S(2)}, u32[]{:S(2)}) %collective-permute-start) | collective-permute-done | bytes 524320 | tf_op jit(solution)/shard_map/ppermute | solution.py:137
  614.9 1.9 copy.118
  (100 shorter events, 13.2 us)
Async XLA Ops:
  7.2 128.0 %copy-start = (bf16[16,32768]{1,0:T(8,128)(2,1)S(1)}, bf16[16,32768]{1,0:T(8,128)(2,1)}, u32[]{:S(2)}) copy-start(bf16[16,32768]{1,0:T(8,128)(2,1)} %param.17) | copy-start | bytes 3145732
  7.2 63.8 %all-gather.4.cloned.1.call-start = ((), (), s32[]{:S(2)}) async-start(), calls=%async_computation.9 | async-start | bytes 4718592 | tf_op jit(solution)/shard_map/all_gather | solution.py:41
  34.3 133.4 %reduce-scatter.4.cloned.1.call-start = ((), (), s32[]{:S(2)}) async-start(), calls=%async_computation.10 | async-start | bytes 5242880 | tf_op jit(solution)/shard_map/reduce_scatter | solution.py:86
  84.8 156.8 %reduce-scatter.6.cloned.1.call-start = ((), (), s32[]{:S(2)}) async-start(), calls=%async_computation.11 | async-start | bytes 5242880 | tf_op jit(solution)/shard_map/reduce_scatter | solution.py:86
  98.7 0.7 copy-start.10
  98.7 1.7 copy-start.2
  98.7 7.1 %copy-start.12 = (u32[32]{0:T(128)S(1)}, u32[32]{0:T(128)}, u32[]{:S(2)}) copy-start(u32[32]{0:T(128)} %constant.104) | copy-start | bytes 388
  98.7 10.0 %copy-start.11 = (s32[1,1,4,4]{3,2,1,0:T(4,128)S(1)}, s32[1,1,4,4]{3,2,1,0:T(4,128)}, u32[]{:S(2)}) copy-start(s32[1,1,4,4]{3,2,1,0:T(4,128)} %param.15) | copy-start | bytes 196
  101.9 6.9 %all-to-all-start.1 = ((s32[2,1,8]{2,1,0:T(1,128)}), s32[2,1,8]{2,1,0:T(1,128)S(1)}, u32[]{:S(2)}, u32[]{:S(2)}) async-start(s32[2,1,8]{2,1,0:T(1,128)} %bitcast.8), calls=%async_computation.2 | async-start | bytes 2048 | tf_op jit(solution)/shard_map/all_to_all | solution.py:57
  113.6 29.4 %all-to-all-start.4 = ((bf16[4,4,32768]{2,1,0:T(4,128)(2,1)}), bf16[4,4,32768]{2,1,0:T(4,128)(2,1)}, u32[]{:S(2)}, u32[]{:S(2)}) async-start(bf16[4,4,32768]{2,1,0:T(4,128)(2,1)} %bitcast.20), calls=%async_computation.5 | async-start | bytes 2097152 | tf_op jit(solution)/shard_map/all_to_all | solution.py:59
  143.0 16.2 %all-to-all-start.3 = ((bf16[2,8,32768]{2,1,0:T(8,128)(2,1)}), bf16[2,8,32768]{2,1,0:T(8,128)(2,1)S(1)}, u32[]{:S(2)}, u32[]{:S(2)}) async-start(bf16[2,8,32768]{2,1,0:T(8,128)(2,1)} %bitcast.18), calls=%async_computation.4 | async-start | bytes 2097152 | tf_op jit(solution)/shard_map/all_to_all | solution.py:56
  146.6 182.6 %all-gather.8.cloned.1.call-start = ((), (), s32[]{:S(2)}) async-start(), calls=%async_computation.13 | async-start | bytes 5242880 | tf_op jit(solution)/shard_map/all_gather | solution.py:111
  161.0 3.3 copy-start.5
  165.1 76.5 %copy-start.7 = (f32[16,256,128]{2,0,1:T(8,128)S(1)}, f32[16,256,128]{2,0,1:T(8,128)}, u32[]{:S(2)}) copy-start(f32[16,256,128]{2,0,1:T(8,128)} %fusion.13) | copy-start | bytes 6291460
  247.7 162.2 %all-gather.6.cloned.1.call-start = ((), (), s32[]{:S(2)}) async-start(), calls=%async_computation.12 | async-start | bytes 5242880 | tf_op jit(solution)/shard_map/all_gather | solution.py:110
  248.3 265.1 %all-reduce.4.cloned.1.call-start = ((), (), s32[]{:S(2)}) async-start(), calls=%async_computation.15 | async-start | bytes 2097152 | tf_op jit(solution)/shard_map/psum | solution.py:147
  415.1 7.3 %copy-start.6 = (bf16[4,8,128,128]{3,2,1,0:T(8,128)(2,1)S(1)}, bf16[4,8,128,128]{3,2,1,0:T(8,128)(2,1)}, u32[]{:S(2)}) copy-start(bf16[4,8,128,128]{3,2,1,0:T(8,128)(2,1)} %copy-done.5) | copy-start | bytes 3145732
  422.4 11.6 %copy-start.3 = (bf16[32,1024,128]{2,1,0:T(8,128)(2,1)S(1)}, bf16[32,1024,128]{2,1,0:T(8,128)(2,1)}, u32[]{:S(2)}) copy-start(bf16[32,1024,128]{2,1,0:T(8,128)(2,1)} %gather_fusion.3) | copy-start | bytes 25165828
  422.4 11.6 %copy-start.9 = (bf16[16,1024,128]{2,1,0:T(8,128)(2,1)S(1)}, bf16[16,1024,128]{2,1,0:T(8,128)(2,1)}, u32[]{:S(2)}) copy-start(bf16[16,1024,128]{2,1,0:T(8,128)(2,1)} %gather_fusion.5) | copy-start | bytes 12582916
  441.0 142.3 %reduce-scatter.8.cloned.1.call-start = ((), (), s32[]{:S(2)}) async-start(), calls=%async_computation.14 | async-start | bytes 9437184 | tf_op jit(solution)/shard_map/reduce_scatter | solution.py:130
  451.0 8.0 %copy-start.8 = (bf16[1024,2048]{1,0:T(8,128)(2,1)S(1)}, bf16[1024,2048]{1,0:T(8,128)(2,1)}, u32[]{:S(2)}) copy-start(bf16[1024,2048]{1,0:T(8,128)(2,1)} %all-gather.6.cloned.1.call-done) | copy-start | bytes 12582916
  459.0 13.5 %copy-start.4 = (f32[4,16,256,128]{3,1,2,0:T(8,128)S(1)}, f32[4,16,256,128]{3,1,2,0:T(8,128)}, u32[]{:S(2)}) copy-start(f32[4,16,256,128]{3,1,2,0:T(8,128)} %fusion) | copy-start | bytes 25165828
  513.4 76.7 %all-to-all-start.5 = ((bf16[2,8,32768]{2,1,0:T(8,128)(2,1)}), bf16[2,8,32768]{2,1,0:T(8,128)(2,1)S(1)}, u32[]{:S(2)}, u32[]{:S(2)}) async-start(bf16[2,8,32768]{2,1,0:T(8,128)(2,1)} %all-reduce.4.cloned.1.call-done), calls=%async_computation.8 | async-start | bytes 2097152 | tf_op jit(solution)/shard_map/all_to_all | solution.py:148
  585.4 29.5 %collective-permute-start = (bf16[256,1024]{1,0:T(8,128)(2,1)}, bf16[256,1024]{1,0:T(8,128)(2,1)}, u32[]{:S(2)}, u32[]{:S(2)}) collective-permute-start(bf16[256,1024]{1,0:T(8,128)(2,1)} %convert_bitcast_fusion), channel_id=1, source_target_pairs={{0,0},{1,8},{2,16},{3,24},{8,1},{9,9},{10,17},{11,25},{16,2},{17,1... | collective-permute-start | bytes 1572872 | tf_op jit(solution)/shard_map/ppermute | solution.py:137
  590.1 26.6 %copy-start.1 = (bf16[16,32768]{1,0:T(8,128)(2,1)S(1)}, bf16[16,32768]{1,0:T(8,128)(2,1)}, u32[]{:S(2)}) copy-start(bf16[16,32768]{1,0:T(8,128)(2,1)} %param.17) | copy-start | bytes 3145732
Sparse Core Ops, SparseCore 0:
  34.4 36.5 all-gather.3
  84.9 76.9 reduce-scatter.3
  164.3 77.2 reduce-scatter.5
  247.8 81.2 all-gather.7
  330.6 79.2 all-gather.5
  441.1 50.2 all-reduce.3
  513.5 69.7 reduce-scatter.7

commit v2 on v1

--- a/solution.py
+++ b/solution.py
@@ -81,11 +81,20 @@
     safe = jnp.where(cells >= 0, cells, 0)
     row_of, col_of = safe // slab_width, safe % slab_width
 
-    def frozen(weights):
-        partial = jnp.dot(x_all, weights, preferred_element_type=F32).astype(BF16)
-        return lax.psum_scatter(partial, "dp", scatter_dimension=0, tiled=True).astype(F32)
-
-    gate_frozen, up_frozen = frozen(gate_base), frozen(up_base)
+    half = slab_cols // 2
+
+    def frozen(part_index):
+        cols = slice(part_index * half, (part_index + 1) * half)
+        partial = jnp.concatenate(
+            [
+                jnp.dot(x_all, gate_base[:, cols], preferred_element_type=F32).astype(BF16),
+                jnp.dot(x_all, up_base[:, cols], preferred_element_type=F32).astype(BF16),
+            ],
+            axis=1,
+        )
+        return lax.psum_scatter(partial, "dp", scatter_dimension=0, tiled=True)
+
+    first, second = frozen(0), frozen(1)
 
     x_slots = tokens_in.reshape(group_rows, row_blocks, BLK).transpose(1, 0, 2)[row_of]
     counted_here = lax.dynamic_index_in_dim(counted, part, 1, keepdims=False)
@@ -101,14 +110,50 @@
         placed = jnp.einsum("kc,ktj->ctj", to_cols, products, preferred_element_type=F32)
         return placed.transpose(1, 0, 2).reshape(group_rows, slab_cols)
 
-    gate_pre = gate_frozen + blocks_part(gate_tiles)
-    up_pre = up_frozen + blocks_part(up_tiles)
-    sigmoid_g = jax.nn.sigmoid(gate_pre)
-    upstream = cotangent.astype(F32)
-    d_gate = (upstream * up_pre * sigmoid_g * (1.0 + gate_pre * (1.0 - sigmoid_g))).astype(BF16)
-    d_up = (upstream * gate_pre * sigmoid_g).astype(BF16)
-    g_all = lax.all_gather(d_gate, "dp", axis=0, tiled=True)
-    u_all = lax.all_gather(d_up, "dp", axis=0, tiled=True)
+    gate_blocks, up_blocks = blocks_part(gate_tiles), blocks_part(up_tiles)
+
+    def gradients(sums, part_index):
+        cols = slice(part_index * half, (part_index + 1) * half)
+        gate_pre = sums[:, :half].astype(F32) + gate_blocks[:, cols]
+        up_pre = sums[:, half:].astype(F32) + up_blocks[:, cols]
+        sigmoid_g = jax.nn.sigmoid(gate_pre)
+        upstream = cotangent[:, cols].astype(F32)
+        d_gate = upstream * up_pre * sigmoid_g * (1.0 + gate_pre * (1.0 - sigmoid_g))
+        d_up = upstream * gate_pre * sigmoid_g
+        return jnp.concatenate([d_gate.astype(BF16), d_up.astype(BF16)], axis=1)
+
+    d_first = gradients(first, 0)
+    to_right = [(g, g + 1) for g in range(groups - 1)]
+    to_left = [(g + 1, g) for g in range(groups - 1)]
+    from_left, from_right = [d_first], [d_first]
+    for _ in range(groups - 1):
+        from_left.append(lax.ppermute(from_left[-1], "dp", to_right))
+        from_right.append(lax.ppermute(from_right[-1], "dp", to_left))
+    ordered = []
+    for g in range(groups):
+        value = d_first
+        for distance in range(1, groups):
+            value = jnp.where(part - g == distance, from_left[distance], value)
+            value = jnp.where(g - part == distance, from_right[distance], value)
+        ordered.append(value)
+    all_first = jnp.concatenate(ordered, axis=0)
+    contract = (((1,), (1,)), ((), ()))
+
+    def frozen_back(d_all, part_index):
+        cols = slice(part_index * half, (part_index + 1) * half)
+        gate_term = lax.dot_general(
+            d_all[:, :half], gate_base[:, cols], contract, preferred_element_type=F32
+        )
+        return gate_term + lax.dot_general(
+            d_all[:, half:], up_base[:, cols], contract, preferred_element_type=F32
+        )
+
+    all_first, second = lax.optimization_barrier((all_first, second))
+    all_second = lax.all_gather(gradients(second, 1), "dp", axis=0, tiled=True)
+    total_first = frozen_back(all_first, 0)
+    total_first, all_second = lax.optimization_barrier((total_first, all_second))
+    g_all = jnp.concatenate([all_first[:, :half], all_second[:, :half]], axis=1)
+    u_all = jnp.concatenate([all_first[:, half:], all_second[:, half:]], axis=1)
 
     tokens = groups * group_rows
     g_slots = g_all.reshape(tokens, slab_width, BLK).transpose(1, 0, 2)[col_of]
@@ -120,19 +165,19 @@
     products = products + jnp.einsum("ktj,kij->kti", u_slots, up_tiles, preferred_element_type=F32)
     products = products.astype(BF16).reshape(-1, groups, group_rows, BLK)
     placed = jnp.einsum("kgr,kgti->grti", to_rows, products, preferred_element_type=F32)
-    contract = (((1,), (1,)), ((), ()))
-    total = lax.dot_general(g_all, gate_base, contract, preferred_element_type=F32)
-    total = total + lax.dot_general(u_all, up_base, contract, preferred_element_type=F32)
-    total = total + placed.transpose(0, 2, 1, 3).reshape(tokens, own_rows)
+    total = total_first + frozen_back(all_second, 1)
+    total = (total + placed.transpose(0, 2, 1, 3).reshape(tokens, own_rows)).astype(BF16)
 
     out_cols = own_rows // fsdp_ways
     total = total.reshape(groups, group_rows, fsdp_ways, out_cols).transpose(0, 2, 1, 3)
-    summed = lax.psum_scatter(
+    terms = lax.all_to_all(
         total.reshape(plane, group_rows, out_cols),
         ("lang", "fsdp"),
-        scatter_dimension=0,
+        split_axis=0,
+        concat_axis=0,
         tiled=True,
-    )[0].astype(BF16)
+    )
+    summed = jnp.sum(terms.astype(F32), axis=0).astype(BF16)
     swap = [(l * groups + p, p * groups + l) for l in range(lang_ways) for p in range(groups)]
     grad_input = lax.ppermute(summed, ("lang", "dp"), swap)
 

time: 633 us -> 642 us (1.014)
  waiting for transfers between devices: 339 us -> 254 us
  starting transfers between devices: 22.5 us -> 64.3 us
  other arithmetic: 15.8 us -> 37.9 us
  matrix products: 102 us -> 121 us
  local copies, waits for them, and re-layouts: 96.4 us -> 109 us
    reduce_scatter x3 -> x2, waiting for transfers between devices: 140 us -> 0.01 us  [frozen(): return lax.psum_scatter(partial, 'dp', scatter_dimension=0, tiled=True)]
    ppermute x0 -> x6, waiting for transfers between devices: none -> 104 us  [the longest x3 93.3 us: on_device(): from_left.append(lax.ppermute(from_left[-1], 'dp', to_right))]
    all_gather x2 -> x1, waiting for transfers between devices: 130 us -> 38 us  [on_device(): all_second = lax.all_gather(gradients(second, 1), 'dp', axis=0, tiled=True)]
    psum x1, waiting for transfers between devices: 0.02 us -> 52.3 us  [on_device(): slot_grads = lax.psum(slot_grads, 'dp')]
    ppermute x0 -> x6, starting transfers between devices: none -> 34.4 us  [the longest x3 30.6 us: on_device(): from_left.append(lax.ppermute(from_left[-1], 'dp', to_right))]
    dot_general x4 -> x8, matrix products: 61.1 us -> 79.3 us  [the longest x2 28 us: frozen_back(): lax.dot_general(d_all[:, half:], up_base[:, cols], contract, preferred_el...]
    concatenate x0 -> x7, other arithmetic: none -> 15.1 us  [the longest x2 4.88 us: frozen(): jnp.concatenate([jnp.dot(x_all, gate_base[:, cols], preferred_element_typ...]
    transpose x3 -> x2, local copies, waits for them, and re-layouts: 19.6 us -> 4.71 us  [blocks_part(): return placed.transpose(1, 0, 2).reshape(group_rows, slab_cols)]
  transfers between devices with their start and end apart: 12 -> 18, of which waited for: 8 -> 12; matrix products, arithmetic and copies ran while one was open for 25% -> 19% of each run, Pallas kernels for 0% -> 0%
where the time goes in v2:
time: 642 us; the launch traced here: 632 us
  waiting for transfers between devices  254 us (40%)
  matrix products  121 us (19%)
  local copies, waits for them, and re-layouts  109 us (17%)
  starting transfers between devices  64.3 us (10%)
  other arithmetic  37.9 us (6%)
  blocking collectives  29.7 us (5%)
  between operations  15.5 us (2%)
    ppermute x3, waiting for transfers between devices, on_device(): from_left.append(lax.ppermute(from_left[-1], 'dp', to_right))  93.3 us
    psum x1, waiting for transfers between devices, on_device(): slot_grads = lax.psum(slot_grads, 'dp')  52.3 us
    all_gather x1, waiting for transfers between devices, on_device(): all_second = lax.all_gather(gradients(second, 1), 'dp', axis=0, tiled=True)  38 us
    all_gather x1, waiting for transfers between devices, on_device(): lax.all_gather(mine.reshape(groups * group_rows, piece), ('lang', 'fsdp')...  36.6 us
    ppermute x3, starting transfers between devices, on_device(): from_left.append(lax.ppermute(from_left[-1], 'dp', to_right))  30.6 us
    dot_general x2, matrix products, frozen_back(): lax.dot_general(d_all[:, half:], up_base[:, cols], contract, preferred_el...  28 us
    all_to_all x1, blocking collectives, on_device(): mine = lax.all_to_all(mine, 'dp', split_axis=1, concat_axis=0, tiled=True)  19.3 us
    dot_general x2, matrix products, frozen_back(): lax.dot_general(d_all[:, :half], gate_base[:, cols], contract, preferred_...  18.5 us
  transfers between devices with their start and end apart: 18, of which 12 were waited for; matrix products, arithmetic and copies ran while one was open for 19% of the time, Pallas kernels for 0%

profile of v2, /device:TPU:2, one launch (start us, length us, event | category | flops | bytes accessed | tf_op | source)
XLA Modules:
  0.0 632.0 jit_solution(11558413610659576161)
XLA Ops:
  7.2 6.5 %copy.90 = bf16[256,8192]{0,1:T(8,128)(2,1)} copy(bf16[256,8192]{1,0:T(8,128)(2,1)} %param.10) | data formatting | bytes 8388608 | tf_op args[0]
  15.0 19.3 %all_to_all.50 = bf16[256,4,256]{2,0,1:T(8,128)(2,1)} all-to-all(bf16[256,4,256]{2,0,1:T(8,128)(2,1)S(1)} %bitcast.127), channel_id=1, replica_groups=mesh['lang'=4,'fsdp'=2,'dp'=4] {'dp'}, dimensions={1} | all-to-all | bytes 1048576 | tf_op jit(solution)/shard_map/all_to_all | solution.py:40
  34.4 36.6 %all-gather.3.cloned.1.call-done = bf16[1024,2048]{1,0:T(8,128)(2,1)} async-done(((bf16[1024,256]{1,0:T(8,128)(2,1)}), bf16[1024,2048]{1,0:T(8,128)(2,1)}) %all-gather.3.cloned.1.call-update) | async-done | bytes 4194320 | tf_op jit(solution)/shard_map/all_gather | solution.py:41
  71.0 8.2 %fusion.28 = bf16[1024,1024]{0,1:T(8,128)(2,1)S(1)} fusion(bf16[1024,2048]{1,0:T(8,128)(2,1)} %all-gather.3.cloned.1.call-done, bf16[2048,2048]{1,0:T(8,128)(2,1)} %param.13), kind=kOutput, calls=%fused_computation.45 | convolution fusion | flops 4296015872 | bytes 10485760 | tf_op jit(solution)/shard_map/dot_general | solution.py:91
  79.2 7.0 %fusion.25 = bf16[1024,1024]{0,1:T(8,128)(2,1)S(1)} fusion(bf16[1024,2048]{1,0:T(8,128)(2,1)S(1)} %copy-done.11, bf16[2048,2048]{1,0:T(8,128)(2,1)} %param.12), kind=kOutput, calls=%fused_computation.44 | convolution fusion | flops 4296015872 | bytes 10485760 | tf_op jit(solution)/shard_map/dot_general | solution.py:90
  97.0 10.4 %all-reduce.1 = s32[4]{0:T(128)S(1)} all-reduce(s32[4]{0:T(128)S(1)} %dynamic-update-slice), channel_id=1, replica_groups=mesh['lang'=4,'fsdp'=2,'dp'=4] {'dp'}, use_global_device_ids=true, to_apply=%add.1 | all-reduce | flops 4 | bytes 32
  109.5 6.4 %copy.95 = bf16[256,64,128]{2,0,1:T(8,128)(2,1)} copy(bf16[256,64,128]{0,2,1:T(8,128)(2,1)} %bitcast.110) | data formatting | bytes 8388608 | tf_op jit(solution)/shard_map/reshape | solution.py:99
  118.2 3.7 all-to-all-start.2
  123.6 5.7 all-to-all-start.4
  133.6 9.4 %fusion.34 = bf16[1024,1024]{0,1:T(8,128)(2,1)} fusion(bf16[1024,2048]{1,0:T(8,128)(2,1)} %all-gather.3.cloned.1.call-done, bf16[2048,2048]{1,0:T(8,128)(2,1)} %param.13), kind=kOutput, calls=%fused_computation.47 | convolution fusion | flops 4296015872 | bytes 10485760 | tf_op jit(solution)/shard_map/dot_general | solution.py:91
  143.0 4.5 all-to-all-start.3
  147.6 8.2 %fusion.31 = bf16[1024,1024]{0,1:T(8,128)(2,1)S(1)} fusion(bf16[1024,2048]{1,0:T(8,128)(2,1)} %all-gather.3.cloned.1.call-done, bf16[2048,2048]{1,0:T(8,128)(2,1)} %param.12), kind=kOutput, calls=%fused_computation.46 | convolution fusion | flops 4296015872 | bytes 10485760 | tf_op jit(solution)/shard_map/dot_general | solution.py:90
  182.5 44.1 %collective-permute-done.3 = bf16[256,2048]{0,1:T(8,128)(2,1)S(1)} collective-permute-done((bf16[256,2048]{0,1:T(8,128)(2,1)S(1)}, bf16[256,2048]{0,1:T(8,128)(2,1)S(1)}, u32[]{:S(2)}, u32[]{:S(2)}) %collective-permute-start.3) | collective-permute-done | bytes 1048608 | tf_op jit(solution)/shard_map/ppermute | solution.py:130
  226.6 22.9 %collective-permute-start.4 = (bf16[256,2048]{0,1:T(8,128)(2,1)S(1)}, bf16[256,2048]{0,1:T(8,128)(2,1)}, u32[]{:S(2)}, u32[]{:S(2)}) collective-permute-start(bf16[256,2048]{0,1:T(8,128)(2,1)S(1)} %collective-permute-done.3), channel_id=1, source_target_pairs={{0,1},{1,2},{2,3},{4,5},{5,6},{6,7},{8,9},{9,10},{10,11},{12,13},{... | collective-permute-start | bytes 3145736 | tf_op jit(solution)/shard_map/ppermute | solution.py:130
  249.5 5.6 collective-permute-done
  256.4 30.9 %collective-permute-done.4 = bf16[256,2048]{0,1:T(8,128)(2,1)} collective-permute-done((bf16[256,2048]{0,1:T(8,128)(2,1)S(1)}, bf16[256,2048]{0,1:T(8,128)(2,1)}, u32[]{:S(2)}, u32[]{:S(2)}) %collective-permute-start.4) | collective-permute-done | bytes 1048608 | tf_op jit(solution)/shard_map/ppermute | solution.py:130
  287.3 5.5 collective-permute-start.5
  296.2 18.3 %collective-permute-done.5 = bf16[256,2048]{0,1:T(8,128)(2,1)} collective-permute-done((bf16[256,2048]{0,1:T(8,128)(2,1)}, bf16[256,2048]{0,1:T(8,128)(2,1)}, u32[]{:S(2)}, u32[]{:S(2)}) %collective-permute-start.5) | collective-permute-done | bytes 1048608 | tf_op jit(solution)/shard_map/ppermute | solution.py:130
  314.5 5.1 collective-permute-done.2
  331.9 6.5 %copy.105 = bf16[1024,2048]{0,1:T(8,128)(2,1)} copy(bf16[1024,2048]{1,0:T(8,128)(2,1)} %all-gather.3.cloned.1.call-done) | data formatting | bytes 8388608 | tf_op jit(solution)/shard_map/all_gather | solution.py:41
  338.4 6.4 %copy.106 = bf16[1024,16,128]{2,0,1:T(8,128)(2,1)} copy(bf16[1024,16,128]{0,2,1:T(8,128)(2,1)} %bitcast.116) | data formatting | bytes 8388608 | tf_op jit(solution)/shard_map/reshape | solution.py:186
  344.9 5.2 gather_fusion.5
  350.1 4.2 fusion.89
  354.2 9.4 %fusion.17 = f32[1024,2048]{1,0:T(8,128)} fusion(bf16[2048,2048]{1,0:T(8,128)(2,1)} %param.12, bf16[1024,2048]{0,1:T(8,128)(2,1)S(1)} %copy-done.4), kind=kOutput, calls=%fused_computation.32 | convolution fusion | flops 4294967296 | bytes 14680064 | tf_op jit(solution)/shard_map/dot_general | solution.py:144
  363.6 9.0 %convolution_add_fusion = f32[1024,2048]{1,0:T(8,128)} fusion(f32[1024,2048]{1,0:T(8,128)} %fusion.17, bf16[2048,2048]{1,0:T(8,128)(2,1)S(1)} %bitcast.134, bf16[1024,2048]{0,1:T(8,128)(2,1)S(1)} %copy-done.4), kind=kOutput, calls=%fused_computation.21 | convolution fusion | flops 4297064448 | bytes 23068672 | tf_op jit(solution)/shard_map/dot_general | solution.py:147
  372.6 38.0 %all-gather.5.cloned.1.call-done = bf16[1024,2048]{0,1:T(8,128)(2,1)} async-done(((bf16[256,2048]{0,1:T(8,128)(2,1)}), bf16[1024,2048]{0,1:T(8,128)(2,1)}) %all-gather.5.cloned.1.call-update) | async-done | bytes 4194320 | tf_op jit(solution)/shard_map/all_gather | solution.py:152
  410.6 4.2 fusion.90
  414.8 9.2 %fusion.10 = f32[1024,2048]{1,0:T(8,128)} fusion(bf16[2048,2048]{1,0:T(8,128)(2,1)} %param.12, bf16[1024,2048]{0,1:T(8,128)(2,1)S(1)} %copy-done.12), kind=kOutput, calls=%fused_computation.25 | convolution fusion | flops 4294967296 | bytes 14680064 | tf_op jit(solution)/shard_map/dot_general | solution.py:144
  426.4 6.4 %copy.102 = bf16[1024,16,128]{2,0,1:T(8,128)(2,1)} copy(bf16[1024,16,128]{0,2,1:T(8,128)(2,1)} %bitcast.114) | data formatting | bytes 8388608 | tf_op jit(solution)/shard_map/reshape | solution.py:160
  432.8 4.0 pad_maximum_fusion.3
  436.8 6.4 %copy.101 = bf16[1024,16,128]{2,0,1:T(8,128)(2,1)} copy(bf16[1024,16,128]{0,2,1:T(8,128)(2,1)} %bitcast.115) | data formatting | bytes 8388608 | tf_op jit(solution)/shard_map/reshape | solution.py:159
  443.2 7.5 %gather_fusion.3 = bf16[32,1024,128]{2,1,0:T(8,128)(2,1)} fusion(bf16[16,1024,128]{2,1,0:T(8,128)(2,1)} %bitcast.108, s32[1024]{0:T(1024)S(1)} %pad_clamp_fusion.1), kind=kCustom, calls=%fused_computation.3 | custom fusion | bytes 16777344 | tf_op jit(solution)/shard_map/gather | solution.py:159
  450.7 11.6 %fusion.92 = f32[32,1024,128]{2,1,0:T(8,128)} fusion(bf16[32,1024,128]{2,1,0:T(8,128)(2,1)} %gather_fusion.3, bf16[32,128,128]{2,1,0:T(8,128)(2,1)S(1)} %bitcast.120), kind=kOutput, calls=%fused_computation.155 | convolution fusion | flops 1073741824 | bytes 26214400 | tf_op jit(solution)/shard_map/ktj,kij->kti/dot_general | solution.py:164
  463.7 7.2 %gather_fusion.4 = bf16[32,1024,128]{2,1,0:T(8,128)(2,1)} fusion(bf16[16,1024,128]{2,1,0:T(8,128)(2,1)} %bitcast.107, s32[1024]{0:T(1024)S(1)} %pad_clamp_fusion.1), kind=kCustom, calls=%fused_computation.4 | custom fusion | bytes 16777344 | tf_op jit(solution)/shard_map/gather | solution.py:160
  470.9 4.8 fusion.46
  477.2 9.7 %add_convert_fusion = bf16[32,1024,128]{2,1,0:T(8,128)(2,1)S(1)} fusion(f32[32,1024,128]{2,1,0:T(8,128)} %fusion.92, bf16[32,1024,128]{2,1,0:T(8,128)(2,1)} %gather_fusion.4, bf16[32,128,128]{2,1,0:T(8,128)(2,1)S(1)} %bitcast.118), kind=kOutput, calls=%fused_computation.7 | convolution fusion | flops 1082130432 | bytes 34603008 | tf_op jit(solution)/shard_map/ktj,kij->kti/dot_general | solution.py:165
  487.0 8.1 %fusion.1 = f32[4,16,256,128]{3,1,2,0:T(8,128)} fusion(bf16[32,4,256,128]{3,2,1,0:T(8,128)(2,1)S(1)} %bitcast.106, pred[32,16]{0,1:T(8,128)(4,1)S(1)} %iota_compare_fusion, pred[32,4]{0,1:T(4,128)(4,1)S(1)} %or_and_fusion), kind=kOutput, calls=%fused_computation.10 | convolution fusion | flops 134219776 | bytes 16777856 | tf_op jit(solution)/shard_map/kgr,kgti->grti/dot_general | solution.py:167
  495.0 19.0 %fusion = bf16[1024,2048]{1,0:T(8,128)(2,1)} fusion(f32[128,8,16,128]{3,2,1,0:T(8,128)} %bitcast.111, f32[1024,2048]{1,0:T(8,128)} %convolution_add_fusion, f32[1024,2048]{1,0:T(8,128)} %fusion.10, bf16[2048,2048]{1,0:T(8,128)(2,1)} %param.13, bf16[1024,2048]{0,1:T(8,128)(2,1)} %all-gather.5.cloned.1.call-done), kind=kOutput, calls=%fused_computation.9 | convolution fusion | flops 4303355904 | bytes 35651584 | tf_op jit(solution)/shard_map/dot_general | solution.py:147
  514.0 8.1 %reshape.506 = bf16[4,256,2,1024]{3,2,1,0:T(2,128)(2,1)} reshape(bf16[1024,2048]{1,0:T(8,128)(2,1)} %fusion) | data formatting | bytes 8388608 | tf_op jit(solution)/shard_map/reshape | solution.py:172
  522.1 5.5 copy.104
  527.5 5.2 all-to-all-start.5
  534.0 52.3 %all-reduce.4.cloned.1.call-done = bf16[2,8,32768]{2,1,0:T(8,128)(2,1)} async-done(((bf16[2,8,32768]{2,1,0:T(8,128)(2,1)}), bf16[2,8,32768]{2,1,0:T(8,128)(2,1)}) %all-reduce.4.cloned.1.call-update) | async-done | bytes 1048592 | tf_op jit(solution)/shard_map/psum | solution.py:192
  586.2 3.6 all-to-all-start.6
  589.8 4.0 reduce_sum.22
  593.8 3.7 collective-permute-start.6
  597.6 6.3 %all-to-all-done.6 = bf16[2,8,32768]{2,1,0:T(8,128)(2,1)S(1)} async-done(((bf16[2,8,32768]{2,1,0:T(8,128)(2,1)}), bf16[2,8,32768]{2,1,0:T(8,128)(2,1)S(1)}, u32[]{:S(2)}, u32[]{:S(2)}) %all-to-all-start.6) | async-done | bytes 1048608 | tf_op jit(solution)/shard_map/all_to_all | solution.py:193
  603.9 3.6 gather_fusion.6
  608.9 14.2 %collective-permute-done.6 = bf16[256,1024]{1,0:T(8,128)(2,1)} collective-permute-done((bf16[256,1024]{1,0:T(8,128)(2,1)}, bf16[256,1024]{1,0:T(8,128)(2,1)}, u32[]{:S(2)}, u32[]{:S(2)}) %collective-permute-start.6) | collective-permute-done | bytes 524320 | tf_op jit(solution)/shard_map/ppermute | solution.py:182
  (155 shorter events, 75.1 us)
Async XLA Ops:
  7.2 108.8 %copy-start = (bf16[16,32768]{1,0:T(8,128)(2,1)S(1)}, bf16[16,32768]{1,0:T(8,128)(2,1)}, u32[]{:S(2)}) copy-start(bf16[16,32768]{1,0:T(8,128)(2,1)} %param.17) | copy-start | bytes 3145732
  7.2 63.8 %all-gather.3.cloned.1.call-start = ((), (), s32[]{:S(2)}) async-start(), calls=%async_computation.9 | async-start | bytes 4718592 | tf_op jit(solution)/shard_map/all_gather | solution.py:41
  34.3 141.9 %reduce-scatter.3.cloned.1.call-start = ((), (), s32[]{:S(2)}) async-start(), calls=%async_computation.10 | async-start | bytes 5242880 | tf_op jit(solution)/shard_map/reduce_scatter | solution.py:95
  71.0 8.2 %copy-start.11 = (bf16[1024,2048]{1,0:T(8,128)(2,1)S(1)}, bf16[1024,2048]{1,0:T(8,128)(2,1)}, u32[]{:S(2)}) copy-start(bf16[1024,2048]{1,0:T(8,128)(2,1)} %all-gather.3.cloned.1.call-done) | copy-start | bytes 12582916
  88.6 0.8 copy-start.17
  88.6 2.4 copy-start.2
  88.6 3.1 copy-start.21
  88.6 19.0 %copy-start.16 = (bf16[256,2048]{1,0:T(8,128)(2,1)S(1)}, bf16[256,2048]{1,0:T(8,128)(2,1)}, u32[]{:S(2)}) copy-start(bf16[256,2048]{1,0:T(8,128)(2,1)} %param.11) | copy-start | bytes 3145732
  89.7 0.5 copy-start.19
  93.8 24.4 %all-to-all-start.1 = ((s32[2,1,8]{2,1,0:T(1,128)}), s32[2,1,8]{2,1,0:T(1,128)S(1)}, u32[]{:S(2)}, u32[]{:S(2)}) async-start(s32[2,1,8]{2,1,0:T(1,128)} %bitcast.8), calls=%async_computation.2 | async-start | bytes 2048 | tf_op jit(solution)/shard_map/all_to_all | solution.py:57
  118.2 5.4 all-to-all-start.2
  123.6 19.4 %all-to-all-start.4 = ((bf16[4,4,32768]{2,1,0:T(4,128)(2,1)}), bf16[4,4,32768]{2,1,0:T(4,128)(2,1)S(1)}, u32[]{:S(2)}, u32[]{:S(2)}) async-start(bf16[4,4,32768]{2,1,0:T(4,128)(2,1)} %bitcast.20), calls=%async_computation.5 | async-start | bytes 2097152 | tf_op jit(solution)/shard_map/all_to_all | solution.py:59
  143.0 18.8 %all-to-all-start.3 = ((bf16[2,8,32768]{2,1,0:T(8,128)(2,1)}), bf16[2,8,32768]{2,1,0:T(8,128)(2,1)}, u32[]{:S(2)}, u32[]{:S(2)}) async-start(bf16[2,8,32768]{2,1,0:T(8,128)(2,1)} %bitcast.18), calls=%async_computation.4 | async-start | bytes 2097152 | tf_op jit(solution)/shard_map/all_to_all | solution.py:56
  147.5 181.0 %reduce-scatter.5.cloned.1.call-start = ((), (), s32[]{:S(2)}) async-start(), calls=%async_computation.11 | async-start | bytes 5242880 | tf_op jit(solution)/shard_map/reduce_scatter | solution.py:95
  147.6 8.3 %copy-start.15 = (bf16[1024,1024]{0,1:T(8,128)(2,1)S(1)}, bf16[1024,1024]{0,1:T(8,128)(2,1)}, u32[]{:S(2)}) copy-start(bf16[1024,1024]{0,1:T(8,128)(2,1)} %fusion.34) | copy-start | bytes 6291460
  158.3 252.3 %all-gather.5.cloned.1.call-start = ((), (), s32[]{:S(2)}) async-start(), calls=%async_computation.12 | async-start | bytes 5242880 | tf_op jit(solution)/shard_map/all_gather | solution.py:152
  163.7 4.6 copy-start.5
  178.9 47.7 %collective-permute-start.3 = (bf16[256,2048]{0,1:T(8,128)(2,1)S(1)}, bf16[256,2048]{0,1:T(8,128)(2,1)S(1)}, u32[]{:S(2)}, u32[]{:S(2)}) collective-permute-start(bf16[256,2048]{0,1:T(8,128)(2,1)S(1)} %pad_maximum_fusion.7), channel_id=1, source_target_pairs={{0,1},{1,2},{2,3},{4,5},{5,6},{6,7},{8,9},{9,10},{10,11},{12,13},{... | collective-permute-start | bytes 3145736 | tf_op jit(solution)/shard_map/ppermute | solution.py:130
  181.2 73.9 %collective-permute-start = (bf16[256,2048]{0,1:T(8,128)(2,1)S(1)}, bf16[256,2048]{0,1:T(8,128)(2,1)S(1)}, u32[]{:S(2)}, u32[]{:S(2)}) collective-permute-start(bf16[256,2048]{0,1:T(8,128)(2,1)S(1)} %pad_maximum_fusion.7), channel_id=1, source_target_pairs={{1,0},{2,1},{3,2},{5,4},{6,5},{7,6},{9,8},{10,9},{11,10},{13,12},{... | collective-permute-start | bytes 3145736 | tf_op jit(solution)/shard_map/ppermute | solution.py:131
  226.6 60.7 %collective-permute-start.4 = (bf16[256,2048]{0,1:T(8,128)(2,1)S(1)}, bf16[256,2048]{0,1:T(8,128)(2,1)}, u32[]{:S(2)}, u32[]{:S(2)}) collective-permute-start(bf16[256,2048]{0,1:T(8,128)(2,1)S(1)} %collective-permute-done.3), channel_id=1, source_target_pairs={{0,1},{1,2},{2,3},{4,5},{5,6},{6,7},{8,9},{9,10},{10,11},{12,13},{... | collective-permute-start | bytes 3145736 | tf_op jit(solution)/shard_map/ppermute | solution.py:130
  255.1 37.7 %collective-permute-start.1 = (bf16[256,2048]{0,1:T(8,128)(2,1)S(1)}, bf16[256,2048]{0,1:T(8,128)(2,1)}, u32[]{:S(2)}, u32[]{:S(2)}) collective-permute-start(bf16[256,2048]{0,1:T(8,128)(2,1)S(1)} %collective-permute-done), channel_id=1, source_target_pairs={{1,0},{2,1},{3,2},{5,4},{6,5},{7,6},{9,8},{10,9},{11,10},{13,12},{... | collective-permute-start | bytes 3145736 | tf_op jit(solution)/shard_map/ppermute | solution.py:131
  287.3 27.2 %collective-permute-start.5 = (bf16[256,2048]{0,1:T(8,128)(2,1)}, bf16[256,2048]{0,1:T(8,128)(2,1)}, u32[]{:S(2)}, u32[]{:S(2)}) collective-permute-start(bf16[256,2048]{0,1:T(8,128)(2,1)} %collective-permute-done.4), channel_id=1, source_target_pairs={{0,1},{1,2},{2,3},{4,5},{5,6},{6,7},{8,9},{9,10},{10,11},{12,13},{... | collective-permute-start | bytes 3145736 | tf_op jit(solution)/shard_map/ppermute | solution.py:130
  292.8 26.8 %collective-permute-start.2 = (bf16[256,2048]{0,1:T(8,128)(2,1)}, bf16[256,2048]{0,1:T(8,128)(2,1)}, u32[]{:S(2)}, u32[]{:S(2)}) collective-permute-start(bf16[256,2048]{0,1:T(8,128)(2,1)} %collective-permute-done.1), channel_id=1, source_target_pairs={{1,0},{2,1},{3,2},{5,4},{6,5},{7,6},{9,8},{10,9},{11,10},{13,12},{... | collective-permute-start | bytes 3145736 | tf_op jit(solution)/shard_map/ppermute | solution.py:131
  325.8 2.7 copy-start.8
  325.8 2.7 copy-start.14
  350.1 4.2 copy-start.4
  350.1 13.5 %slice-start = ((s8[8388608]{0:T(1024)(128)(4,1)}), s8[4194304]{0:T(1024)(128)(4,1)S(1)}, s32[]{:S(2)}) async-start(s8[8388608]{0:T(1024)(128)(4,1)} %bitcast.133), calls=%async_computation.14 | async-start | bytes 8388608
  354.2 9.4 %slice-start.1 = ((s8[8388608]{0:T(1024)(128)(4,1)}), s8[4194304]{0:T(1024)(128)(4,1)S(1)}, s32[]{:S(2)}) async-start(s8[8388608]{0:T(1024)(128)(4,1)} %bitcast.133), calls=%async_computation.15 | async-start | bytes 8388608
  410.6 4.2 copy-start.12
  414.8 9.2 %copy-start.9 = (bf16[1024,1024]{0,1:T(8,128)(2,1)S(1)}, bf16[1024,1024]{0,1:T(8,128)(2,1)}, u32[]{:S(2)}) copy-start(bf16[1024,1024]{0,1:T(8,128)(2,1)} %get-tuple-element.17) | copy-start | bytes 6291460
  443.2 7.5 %copy-start.7 = (bf16[4,8,128,128]{3,2,1,0:T(8,128)(2,1)S(1)}, bf16[4,8,128,128]{3,2,1,0:T(8,128)(2,1)}, u32[]{:S(2)}) copy-start(bf16[4,8,128,128]{3,2,1,0:T(8,128)(2,1)} %copy.117) | copy-start | bytes 3145732
  450.7 11.6 %copy-start.3 = (bf16[32,1024,128]{2,1,0:T(8,128)(2,1)S(1)}, bf16[32,1024,128]{2,1,0:T(8,128)(2,1)}, u32[]{:S(2)}) copy-start(bf16[32,1024,128]{2,1,0:T(8,128)(2,1)} %gather_fusion.3) | copy-start | bytes 25165828
  450.7 11.6 %copy-start.13 = (bf16[16,1024,128]{2,1,0:T(8,128)(2,1)S(1)}, bf16[16,1024,128]{2,1,0:T(8,128)(2,1)}, u32[]{:S(2)}) copy-start(bf16[16,1024,128]{2,1,0:T(8,128)(2,1)} %gather_fusion.5) | copy-start | bytes 12582916
  475.7 1.5 copy-start.6
  527.5 5.2 copy-start.10
  527.5 58.7 %all-to-all-start.5 = ((bf16[8,256,1024]{2,1,0:T(8,128)(2,1)}), bf16[8,256,1024]{2,1,0:T(8,128)(2,1)}, u32[]{:S(2)}, u32[]{:S(2)}) async-start(bf16[8,256,1024]{2,1,0:T(8,128)(2,1)} %bitcast.112), calls=%async_computation.7 | async-start | bytes 8388608 | tf_op jit(solution)/shard_map/all_to_all | solution.py:173
  532.7 53.5 %all-reduce.4.cloned.1.call-start = ((), (), s32[]{:S(2)}) async-start(), calls=%async_computation.13 | async-start | bytes 2097152 | tf_op jit(solution)/shard_map/psum | solution.py:192
  533.9 63.6 %copy-start.18 = (s32[16,1]{0,1:T(1,128)S(1)}, s32[16,1]{0,1:T(1,128)}, u32[]{:S(2)}) copy-start(s32[16,1]{0,1:T(1,128)} %param.18) | copy-start | bytes 196
  533.9 63.6 %copy-start.20 = (s32[16]{0:T(128)S(1)}, s32[16]{0:T(128)}, u32[]{:S(2)}) copy-start(s32[16]{0:T(128)} %copy-done.19) | copy-start | bytes 196
  586.2 17.7 %all-to-all-start.6 = ((bf16[2,8,32768]{2,1,0:T(8,128)(2,1)}), bf16[2,8,32768]{2,1,0:T(8,128)(2,1)S(1)}, u32[]{:S(2)}, u32[]{:S(2)}) async-start(bf16[2,8,32768]{2,1,0:T(8,128)(2,1)} %all-reduce.4.cloned.1.call-done), calls=%async_computation.8 | async-start | bytes 2097152 | tf_op jit(solution)/shard_map/all_to_all | solution.py:193
  593.8 29.3 %collective-permute-start.6 = (bf16[256,1024]{1,0:T(8,128)(2,1)}, bf16[256,1024]{1,0:T(8,128)(2,1)}, u32[]{:S(2)}, u32[]{:S(2)}) collective-permute-start(bf16[256,1024]{1,0:T(8,128)(2,1)} %reduce_sum.22), channel_id=1, source_target_pairs={{0,0},{1,8},{2,16},{3,24},{8,1},{9,9},{10,17},{11,25},{16,2},{17,1... | collective-permute-start | bytes 1572872 | tf_op jit(solution)/shard_map/ppermute | solution.py:182
  603.9 21.1 %copy-start.1 = (bf16[16,32768]{1,0:T(8,128)(2,1)S(1)}, bf16[16,32768]{1,0:T(8,128)(2,1)}, u32[]{:S(2)}) copy-start(bf16[16,32768]{1,0:T(8,128)(2,1)} %param.17) | copy-start | bytes 3145732
Sparse Core Ops, SparseCore 0:
  34.5 36.5 all-gather.2
  88.8 76.9 reduce-scatter.2
  168.1 114.1 reduce-scatter.4
  331.9 78.7 all-gather.4
  536.2 50.0 all-reduce.3
